TPU v7x, 512 devices: a whole 4x4x16 slice. The times are simulated.
512 devices in a mesh: seq: 128 (over z, y, core), ch: 4 (over x).
Axes of the slice: x: 4, y: 4, z: 16, core: 2. Of those that a mesh axis runs over, the one named last changes fastest.
Arguments:
- ingest: bfloat16 [131072, 4096], P('seq', 'ch'), may hold values from -6 to 6
- ingest_count: int32 [128], P('seq'), may hold values from 0 to 1024, as said below
- doc_lengths: int32 [128], replicated, may hold values from 1 to 2048, as said below
- in_weight: bfloat16 [4096, 5120], P('seq', 'ch'), may hold values from -0.09375 to 0.09375
- conv_weight: float32 [4, 5120], P(None, 'ch'), may hold values from -3 to 3
- conv_bias: float32 [5120], P('ch'), may hold values from -3 to 3
Outputs:
- conv_out: bfloat16 [65536, 5120], P('seq', 'ch')
Inputs may be any that keep to these rules, and one draw needn't show every extreme that they name: Device i keeps its valid rows in its first ingest_count[i] slots; the devices before i together hold between i * 512 - 256 and i * 512 + 256 rows, both ends reached in every draw; the first device holds 511 rows, and all devices together hold 65536 rows. `doc_lengths`: the lengths sum to 65536; the first document has exactly 2048 tokens.
All inputs are finite; a program needn't handle non-finite values.
Results may differ from a plain program's by a relative error of at most 0.012.
Values may be sent and summed in bfloat16 or wider, within the bound.
A program may use at most 128 MiB of HBM per device.

v0:
```python
import jax
import jax.numpy as jnp
from jax import lax
from jax.sharding import PartitionSpec as P


def shifted(value, axis, steps):
    count = lax.axis_size(axis)
    initial, last = (max(0, -steps), min(count, count - steps))
    return lax.ppermute(value, axis, [(source, source + steps) for source in range(initial, last)])


def carried_in(value, axis, join, neutral):
    count, mine = (lax.axis_size(axis), lax.axis_index(axis))
    pieces = lax.all_gather(value, axis)
    subtotal = jnp.full_like(value, 0) + jnp.asarray(neutral, value.dtype)

    def turn(position, subtotal):
        longer = join(subtotal, pieces[position])
        return jnp.where(position < mine, longer, subtotal)

    return lax.fori_loop(0, count - 1, turn, subtotal)


def move_rows(ingest, count, offset, first, tokens, extra):
    half = tokens // 2
    slots = ingest.shape[0]
    start = first + tokens - offset - extra
    tail = lax.dynamic_slice_in_dim(ingest, start, half + extra, 0)
    from_left = shifted(tail, "seq", 1)
    from_right = shifted(ingest[:half], "seq", -1)
    next_offset = offset + count
    buffer = jnp.concatenate([from_left, ingest, from_right], axis=0)
    places = first - extra + jnp.arange(tokens + extra, dtype=jnp.int32)
    lead = half + extra
    picks = jnp.where(
        places < offset,
        places - (first - extra),
        jnp.where(
            places < next_offset, lead + places - offset, lead + slots + places - next_offset
        ),
    )
    return jnp.take(buffer, picks.astype(jnp.int32), axis=0)


def body(ingest, ingest_count, doc_lengths, in_weight, conv_weight, conv_bias):
    tokens = ingest.shape[0] // 2
    channels = in_weight.shape[1]
    before = carried_in(
        ingest_count, "seq", lambda earlier, later: earlier + later, jnp.zeros_like(ingest_count)
    )
    offset = before[0]
    count = ingest_count[0]
    first = lax.axis_index("seq") * tokens
    extra = 3
    moved = move_rows(ingest, count, offset, first, tokens, extra)
    features = lax.all_gather(moved, "ch", axis=1, tiled=True)
    window = jnp.dot(
        features,
        lax.all_gather(in_weight, "seq", axis=0, tiled=True),
        preferred_element_type=jnp.float32,
    ).astype(jnp.bfloat16)
    values = window.astype(jnp.float32)
    starts = jnp.cumsum(doc_lengths) - doc_lengths
    places = first - 3 + jnp.arange(tokens + 3, dtype=jnp.int32)
    doc_ids = jnp.sum((places[:, None] >= starts[None, :]).astype(jnp.int32), axis=1) - 1
    here_ids = doc_ids[3:]
    total = jnp.zeros((tokens, channels), jnp.float32) + conv_bias[None, :]
    for lag in range(4):
        earlier = values[3 - lag : 3 - lag + tokens]
        same = (doc_ids[3 - lag : 3 - lag + tokens] == here_ids).astype(jnp.float32)
        total = total + conv_weight[lag][None, :] * earlier * same[:, None]
    return jax.nn.silu(total).astype(jnp.bfloat16)


def solution(mesh):
    placed = (P("seq", "ch"), P("seq"), P(), P("seq", "ch"), P(None, "ch"), P("ch"))
    return jax.shard_map(
        body, mesh=mesh, in_specs=placed, out_specs=P("seq", "ch"), check_vma=False
    )
```

profile of v0, /device:TPU:1, one launch (start us, length us, event | category | flops | bytes accessed | tf_op | source)
XLA Modules:
  0.0 486.9 jit_solution(12569060451620937295)
XLA Ops:
  7.2 1.3 dynamic-slice
  8.5 0.8 dynamic-update-slice
  9.2 30.5 %all-reduce = s32[128]{0:T(128)S(1)} all-reduce(s32[128]{0:T(128)S(1)} %dynamic-update-slice), channel_id=2, replica_groups=mesh['seq'=128,'ch'=4] {'seq'}, use_global_device_ids=true, to_apply=%add | all-reduce | flops 128 | bytes 1024
  39.7 175.2 %while.13 = (s32[]{:T(128)}, s32[1]{0:T(128)}, s32[]{:T(128)}, s32[128,1]{0,1:T(1,128)S(1)}, s32[]{:T(128)}) while((s32[]{:T(128)}, s32[1]{0:T(128)}, s32[]{:T(128)}, s32[128,1]{0,1:T(1,128)S(1)}, s32[]{:T(128)}) %tuple.40), condition=%wide.region_1.2_spmd, body=%wide.region_0.1_spmd.sunk | while | flops 5 | bytes 107 | solution.py:22
  41.1 0.7 constant_dynamic-slice_fusion.3
  42.5 0.7 constant_dynamic-slice_fusion.3
  43.9 0.7 constant_dynamic-slice_fusion.3
  45.3 0.7 constant_dynamic-slice_fusion.3
  46.6 0.7 constant_dynamic-slice_fusion.3
  48.0 0.7 constant_dynamic-slice_fusion.3
  49.4 0.7 constant_dynamic-slice_fusion.3
  50.8 0.7 constant_dynamic-slice_fusion.3
  52.2 0.7 constant_dynamic-slice_fusion.3
  53.5 0.7 constant_dynamic-slice_fusion.3
  54.9 0.7 constant_dynamic-slice_fusion.3
  56.3 0.7 constant_dynamic-slice_fusion.3
  57.7 0.7 constant_dynamic-slice_fusion.3
  59.1 0.7 constant_dynamic-slice_fusion.3
  60.4 0.7 constant_dynamic-slice_fusion.3
  61.8 0.7 constant_dynamic-slice_fusion.3
  63.2 0.7 constant_dynamic-slice_fusion.3
  64.6 0.7 constant_dynamic-slice_fusion.3
  66.0 0.7 constant_dynamic-slice_fusion.3
  67.3 0.7 constant_dynamic-slice_fusion.3
  68.7 0.7 constant_dynamic-slice_fusion.3
  70.1 0.7 constant_dynamic-slice_fusion.3
  71.5 0.7 constant_dynamic-slice_fusion.3
  72.9 0.7 constant_dynamic-slice_fusion.3
  74.2 0.7 constant_dynamic-slice_fusion.3
  75.6 0.7 constant_dynamic-slice_fusion.3
  77.0 0.7 constant_dynamic-slice_fusion.3
  78.4 0.7 constant_dynamic-slice_fusion.3
  79.8 0.7 constant_dynamic-slice_fusion.3
  81.1 0.7 constant_dynamic-slice_fusion.3
  215.0 1.2 constant_dynamic-slice_fusion.1
  216.2 7.4 %collective-permute-start = (bf16[259,1024]{1,0:T(8,128)(2,1)S(1)}, bf16[259,1024]{1,0:T(8,128)(2,1)}, u32[]{:S(2)}, u32[]{:S(2)}) collective-permute-start(bf16[259,1024]{1,0:T(8,128)(2,1)S(1)} %constant_dynamic-slice_fusion.1), channel_id=1, source_target_pairs={{0,4},{4,8},{8,12},{12,16},{16,20},{20,24},{24,28},{28,32},{32,36}... | collective-permute-start | bytes 1591304 | tf_op jit(solution)/shard_map/ppermute | solution.py:10
  223.6 1.1 slice.41
  224.7 2.2 collective-permute-start.1
  227.0 8.2 %collective-permute-done.1 = bf16[256,1024]{1,0:T(8,128)(2,1)S(1)} collective-permute-done((bf16[256,1024]{1,0:T(8,128)(2,1)S(1)}, bf16[256,1024]{1,0:T(8,128)(2,1)S(1)}, u32[]{:S(2)}, u32[]{:S(2)}) %collective-permute-start.1) | collective-permute-done | bytes 524320 | tf_op jit(solution)/shard_map/ppermute | solution.py:10
  235.2 0.8 copy-done
  236.0 14.8 %concatenate.3 = bf16[1539,1024]{1,0:T(8,128)(2,1)S(1)} concatenate(bf16[259,1024]{1,0:T(8,128)(2,1)} %collective-permute-done, bf16[1024,1024]{1,0:T(8,128)(2,1)} %param.8, bf16[256,1024]{1,0:T(8,128)(2,1)} %copy-done), dimensions={0} | concatenate | bytes 6303744 | tf_op jit(solution)/shard_map/concatenate | solution.py:33
  250.8 3.4 gather_fusion
  254.1 2.4 broadcast_select_fusion
  256.6 0.7 all-gather.6.cloned.1.call-update
  258.2 52.7 %all-gather.4.cloned.1.call-done = bf16[515,4096]{1,0:T(8,128)(2,1)} async-done(((bf16[515,1024]{1,0:T(8,128)(2,1)}), bf16[515,4096]{1,0:T(8,128)(2,1)}) %all-gather.4.cloned.1.call-update) | async-done | bytes 4218896 | tf_op jit(solution)/shard_map/all_gather | solution.py:57
  310.8 154.9 %all-gather.6.cloned.1.call-done = bf16[4096,1280]{1,0:T(8,128)(2,1)} async-done(((bf16[32,1280]{1,0:T(8,128)(2,1)}), bf16[4096,1280]{1,0:T(8,128)(2,1)}) %all-gather.6.cloned.1.call-update) | async-done | bytes 10485776 | tf_op jit(solution)/shard_map/all_gather | solution.py:60
  465.8 10.9 %fusion = f32[515,1280]{1,0:T(8,128)S(1)} fusion(bf16[515,4096]{1,0:T(8,128)(2,1)} %all-gather.4.cloned.1.call-done, bf16[4096,1280]{1,0:T(8,128)(2,1)} %all-gather.6.cloned.1.call-done), kind=kOutput, calls=%fused_computation.3 | convolution fusion | flops 5401485312 | bytes 17341440 | tf_op jit(solution)/shard_map/dot_general | solution.py:58
  476.7 3.3 multiply_convert_fusion
  (121 shorter events, 65.4 us)
Async XLA Ops:
  6.5 304.3 %all-gather.4.cloned.1.call-start = ((), (), s32[]{:S(2)}) async-start(), calls=%async_computation | async-start | bytes 5324800 | tf_op jit(solution)/shard_map/all_gather | solution.py:57
  216.2 19.8 %collective-permute-start = (bf16[259,1024]{1,0:T(8,128)(2,1)S(1)}, bf16[259,1024]{1,0:T(8,128)(2,1)}, u32[]{:S(2)}, u32[]{:S(2)}) collective-permute-start(bf16[259,1024]{1,0:T(8,128)(2,1)S(1)} %constant_dynamic-slice_fusion.1), channel_id=1, source_target_pairs={{0,4},{4,8},{8,12},{12,16},{16,20},{20,24},{24,28},{28,32},{32,36}... | collective-permute-start | bytes 1591304 | tf_op jit(solution)/shard_map/ppermute | solution.py:10
  224.7 10.5 %collective-permute-start.1 = (bf16[256,1024]{1,0:T(8,128)(2,1)S(1)}, bf16[256,1024]{1,0:T(8,128)(2,1)S(1)}, u32[]{:S(2)}, u32[]{:S(2)}) collective-permute-start(bf16[256,1024]{1,0:T(8,128)(2,1)S(1)} %slice.41), channel_id=1, source_target_pairs={{4,0},{8,4},{12,8},{16,12},{20,16},{24,20},{28,24},{32,28},{36,32}... | collective-permute-start | bytes 1572872 | tf_op jit(solution)/shard_map/ppermute | solution.py:10
  235.2 0.8 copy-start
  254.1 3.2 copy-start.3
  254.1 3.9 copy-start.1
  256.6 209.2 %all-gather.6.cloned.1.call-start = ((), (), s32[]{:S(2)}) async-start(), calls=%async_computation.1 | async-start | bytes 10567680 | tf_op jit(solution)/shard_map/all_gather | solution.py:60
  258.2 218.6 %copy-start.2 = (f32[1280]{0:T(1024)S(1)}, f32[1280]{0:T(1024)}, u32[]{:S(2)}) copy-start(f32[1280]{0:T(1024)} %param.13) | copy-start | bytes 15364
Sparse Core Ops, SparseCore 0:
  256.7 54.0 all-gather.3
  313.9 151.7 all-gather.5
where the time goes:
time: 489 us; the launch traced here: 487 us
  waiting for transfers between devices  217 us (44%)
  local copies, waits for them, and re-layouts  108 us (22%)
  loops' own time  90.8 us (19%)
  blocking collectives  30.5 us (6%)
  between operations  14.2 us (3%)
  matrix products  10.9 us (2%)
  starting transfers between devices  9.63 us (2%)
  other arithmetic  6.33 us (1%)
    all_gather x1, waiting for transfers between devices, body(): lax.all_gather(in_weight, 'seq', axis=0, tiled=True)  155 us
    another operation x1, loops' own time, carried_in(): return lax.fori_loop(0, count - 1, turn, subtotal)  90.8 us
    dynamic_slice x127, local copies, waits for them, and re-layouts, turn(): longer = join(subtotal, pieces[position])  84.4 us
    all_gather x1, waiting for transfers between devices, body(): features = lax.all_gather(moved, 'ch', axis=1, tiled=True)  52.7 us
    unnamed x1, blocking collectives  30.5 us
    concatenate x1, local copies, waits for them, and re-layouts, move_rows(): buffer = jnp.concatenate([from_left, ingest, from_right], axis=0)  14.8 us
    dot_general x1, matrix products, body(): jnp.dot(features, lax.all_gather(in_weight, 'seq', axis=0, tiled=True), p...  10.9 us
  transfers between devices with their start and end apart: 4, of which 3 were waited for; matrix products, arithmetic and copies ran while one was open for 0% of the time, Pallas kernels for 0%

commit v1 on v0

--- a/solution.py
+++ b/solution.py
@@ -54,7 +54,28 @@
     first = lax.axis_index("seq") * tokens
     extra = 3
     moved = move_rows(ingest, count, offset, first, tokens, extra)
-    features = lax.all_gather(moved, "ch", axis=1, tiled=True)
+    back = lax.axis_size("ch")
+    out_arr = lax.axis_index("ch")
+    reply, right_arr, a_now = (back, out_arr, moved.shape[1])
+    pile = tuple((b * reply if dev == 1 else b for dev, b in enumerate(moved.shape)))
+    block_last = jnp.zeros(pile, moved.dtype)
+    features = lax.dynamic_update_slice_in_dim(block_last, moved, right_arr * a_now, axis=1)
+    q = 1
+    tile_out = z = moved
+    while q < reply // 2 + 1:
+        tile_out = lax.ppermute(
+            tile_out, "ch", tuple(((dev, (dev + 1) % reply) for dev in range(reply)))
+        )
+        features = lax.dynamic_update_slice_in_dim(
+            features, tile_out, (right_arr - q) % reply * a_now, axis=1
+        )
+        if 2 * q < reply:
+            arr_out = tuple(((dev, (dev - 1) % reply) for dev in range(reply)))
+            z = lax.ppermute(z, "ch", arr_out)
+            features = lax.dynamic_update_slice_in_dim(
+                features, z, (right_arr + q) % reply * a_now, axis=1
+            )
+        q += 1
     window = jnp.dot(
         features,
         lax.all_gather(in_weight, "seq", axis=0, tiled=True),

time: 489 us -> 305 us (0.62)
  the two profiles are of different devices: /device:TPU:1 before, /device:TPU:8 now
where the time goes in v1:
time: 305 us; the launch traced here: 304 us
  local copies, waits for them, and re-layouts  101 us (33%)
  loops' own time  72.9 us (24%)
  waiting for transfers between devices  52.5 us (17%)
  blocking collectives  33.3 us (11%)
  starting transfers between devices  14.8 us (5%)
  between operations  14.3 us (5%)
  matrix products  11 us (4%)
  other arithmetic  4.19 us (1%)
    another operation x1, loops' own time, carried_in(): return lax.fori_loop(0, count - 1, turn, subtotal)  72.9 us
    dynamic_slice x127, local copies, waits for them, and re-layouts, turn(): longer = join(subtotal, pieces[position])  70.7 us
    ppermute x2, waiting for transfers between devices, body(): lax.ppermute(tile_out, 'ch', tuple(((dev, (dev + 1) % reply) for dev in r...  45.2 us
    unnamed x1, blocking collectives  33.3 us
    concatenate x1, local copies, waits for them, and re-layouts, move_rows(): buffer = jnp.concatenate([from_left, ingest, from_right], axis=0)  14.8 us
    dot_general x1, matrix products, body(): jnp.dot(features, lax.all_gather(in_weight, 'seq', axis=0, tiled=True), p...  11 us
    ppermute x2, waiting for transfers between devices, shifted(): lax.ppermute(value, axis, [(source, source + steps) for source in range(i...  6.61 us
  transfers between devices with their start and end apart: 6, of which 3 were waited for; matrix products, arithmetic and copies ran while one was open for 32% of the time, Pallas kernels for 0%

profile of v1, /device:TPU:8, one launch (start us, length us, event | category | flops | bytes accessed | tf_op | source)
XLA Modules:
  0.0 303.5 jit_solution(6760010855145460539)
XLA Ops:
  6.5 0.7 all-gather.3.cloned.1.call-update
  7.9 1.2 dynamic-slice
  9.2 0.7 dynamic-update-slice
  9.8 33.3 %all-reduce = s32[128]{0:T(128)S(1)} all-reduce(s32[128]{0:T(128)S(1)} %dynamic-update-slice), channel_id=2, replica_groups=mesh['seq'=128,'ch'=4] {'seq'}, use_global_device_ids=true, to_apply=%add | all-reduce | flops 128 | bytes 1024
  43.1 143.6 %while.13 = (s32[]{:T(128)}, s32[1]{0:T(128)}, s32[]{:T(128)}, s32[128,1]{0,1:T(1,128)S(1)}, s32[]{:T(128)}) while((s32[]{:T(128)}, s32[1]{0:T(128)}, s32[]{:T(128)}, s32[128,1]{0,1:T(1,128)S(1)}, s32[]{:T(128)}) %tuple.39), condition=%wide.region_1.2_spmd, body=%wide.region_0.1_spmd.sunk | while | flops 5 | bytes 107 | solution.py:22
  44.2 0.6 constant_dynamic-slice_fusion.3
  45.4 0.6 constant_dynamic-slice_fusion.3
  46.5 0.6 constant_dynamic-slice_fusion.3
  47.6 0.6 constant_dynamic-slice_fusion.3
  48.8 0.6 constant_dynamic-slice_fusion.3
  49.9 0.6 constant_dynamic-slice_fusion.3
  51.0 0.6 constant_dynamic-slice_fusion.3
  52.2 0.6 constant_dynamic-slice_fusion.3
  53.3 0.6 constant_dynamic-slice_fusion.3
  54.4 0.6 constant_dynamic-slice_fusion.3
  55.5 0.6 constant_dynamic-slice_fusion.3
  68.0 0.6 constant_dynamic-slice_fusion.3
  71.4 0.6 constant_dynamic-slice_fusion.3
  89.5 0.6 constant_dynamic-slice_fusion.3
  92.9 0.6 constant_dynamic-slice_fusion.3
  107.6 0.6 constant_dynamic-slice_fusion.3
  125.6 0.6 constant_dynamic-slice_fusion.3
  142.6 0.6 constant_dynamic-slice_fusion.3
  146.0 0.6 constant_dynamic-slice_fusion.3
  159.6 0.6 constant_dynamic-slice_fusion.3
  163.0 0.6 constant_dynamic-slice_fusion.3
  181.0 0.6 constant_dynamic-slice_fusion.3
  184.4 0.6 constant_dynamic-slice_fusion.3
  186.7 1.2 constant_dynamic-slice_fusion.1
  187.9 1.9 collective-permute-start
  189.8 1.1 slice.41
  190.9 3.6 %collective-permute-start.1 = (bf16[256,1024]{1,0:T(8,128)(2,1)S(1)}, bf16[256,1024]{1,0:T(8,128)(2,1)S(1)}, u32[]{:S(2)}, u32[]{:S(2)}) collective-permute-start(bf16[256,1024]{1,0:T(8,128)(2,1)S(1)} %slice.41), channel_id=1, source_target_pairs={{4,0},{8,4},{12,8},{16,12},{20,16},{24,20},{28,24},{32,28},{36,32}... | collective-permute-start | bytes 1572872 | tf_op jit(solution)/shard_map/ppermute | solution.py:10
  194.6 6.6 %collective-permute-done.1 = bf16[256,1024]{1,0:T(8,128)(2,1)S(1)} collective-permute-done((bf16[256,1024]{1,0:T(8,128)(2,1)S(1)}, bf16[256,1024]{1,0:T(8,128)(2,1)S(1)}, u32[]{:S(2)}, u32[]{:S(2)}) %collective-permute-start.1) | collective-permute-done | bytes 524320 | tf_op jit(solution)/shard_map/ppermute | solution.py:10
  201.2 0.8 copy-done.2
  202.0 14.8 %concatenate.3 = bf16[1539,1024]{1,0:T(8,128)(2,1)S(1)} concatenate(bf16[259,1024]{1,0:T(8,128)(2,1)} %collective-permute-done, bf16[1024,1024]{1,0:T(8,128)(2,1)} %param.8, bf16[256,1024]{1,0:T(8,128)(2,1)} %copy-done.2), dimensions={0} | concatenate | bytes 6303744 | tf_op jit(solution)/shard_map/concatenate | solution.py:33
  216.8 3.4 %gather_fusion = bf16[515,1024]{1,0:T(8,128)(2,1)} fusion(bf16[1539,1024]{1,0:T(8,128)(2,1)S(1)} %concatenate.3, s32[1024]{0:T(1024)S(1)} %pad_clamp_fusion), kind=kCustom, calls=%fused_computation | custom fusion | bytes 2111500 | tf_op jit(solution)/shard_map/jit(_take)/gather | solution.py:43
  220.7 0.7 copy-done
  221.7 2.1 copy-done.1
  223.8 3.4 %collective-permute-start.2 = (bf16[515,1024]{1,0:T(8,128)(2,1)S(1)}, bf16[515,1024]{1,0:T(8,128)(2,1)S(1)}, u32[]{:S(2)}, u32[]{:S(2)}) collective-permute-start(bf16[515,1024]{1,0:T(8,128)(2,1)S(1)} %get-tuple-element.98), channel_id=1, source_target_pairs={{0,1},{1,2},{2,3},{3,0},{4,5},{5,6},{6,7},{7,4},{8,9},{9,10},{10,1... | collective-permute-start | bytes 3164168 | tf_op jit(solution)/shard_map/ppermute | solution.py:66
  227.2 3.6 %collective-permute-start.3 = (bf16[515,1024]{1,0:T(8,128)(2,1)S(1)}, bf16[515,1024]{1,0:T(8,128)(2,1)S(1)}, u32[]{:S(2)}, u32[]{:S(2)}) collective-permute-start(bf16[515,1024]{1,0:T(8,128)(2,1)S(1)} %get-tuple-element.98), channel_id=1, source_target_pairs={{0,3},{1,0},{2,1},{3,2},{4,7},{5,4},{6,5},{7,6},{8,11},{9,8},{10,9... | collective-permute-start | bytes 3164168 | tf_op jit(solution)/shard_map/ppermute | solution.py:74
  231.3 21.7 %collective-permute-done.2 = bf16[515,1024]{1,0:T(8,128)(2,1)S(1)} collective-permute-done((bf16[515,1024]{1,0:T(8,128)(2,1)S(1)}, bf16[515,1024]{1,0:T(8,128)(2,1)S(1)}, u32[]{:S(2)}, u32[]{:S(2)}) %collective-permute-start.2) | collective-permute-done | bytes 1054752 | tf_op jit(solution)/shard_map/ppermute | solution.py:66
  253.0 2.2 collective-permute-start.4
  255.6 1.1 constant_dynamic-update-slice_fusion.2
  256.7 1.1 constant_dynamic-update-slice_fusion.1
  257.8 23.6 %collective-permute-done.4 = bf16[515,1024]{1,0:T(8,128)(2,1)S(1)} collective-permute-done((bf16[515,1024]{1,0:T(8,128)(2,1)S(1)}, bf16[515,1024]{1,0:T(8,128)(2,1)S(1)}, u32[]{:S(2)}, u32[]{:S(2)}) %collective-permute-start.4) | collective-permute-done | bytes 1054752 | tf_op jit(solution)/shard_map/ppermute | solution.py:66
  281.4 1.1 constant_dynamic-update-slice_fusion
  282.4 11.0 %fusion = f32[515,1280]{1,0:T(8,128)S(1)} fusion(bf16[515,4096]{1,0:T(8,128)(2,1)} %constant_dynamic-update-slice_fusion, bf16[4096,1280]{1,0:T(8,128)(2,1)} %all-gather.3.cloned.1.call-done), kind=kOutput, calls=%fused_computation.3 | convolution fusion | flops 5401485312 | bytes 17341440 | tf_op jit(solution)/shard_map/dot_general | solution.py:79
  293.4 3.3 %multiply_convert_fusion = bf16[512,1280]{1,0:T(8,128)(2,1)} fusion(f32[515,1280]{1,0:T(8,128)S(1)} %fusion, f32[512]{0:T(512)S(1)} %get-tuple-element.101, f32[1280]{0:T(1024)S(1)} %get-tuple-element.87, f32[512]{0:T(512)S(1)} %get-tuple-element.100, f32[1280]{0:T(1024)S(1)} %get-tuple-element.88, f32[512]{0:T(512)S(1)} %get-tuple-element.99, ...), kind=kLoop, calls=%fused_computation.15 | loop fusion | flops 10485760 | bytes 11828224 | tf_op jit(solution)/shard_map/convert_element_type | solution.py:94
  (132 shorter events, 59.5 us)
Async XLA Ops:
  6.5 275.9 %all-gather.3.cloned.1.call-start = ((), (), s32[]{:S(2)}) async-start(), calls=%async_computation | async-start | bytes 10567680 | tf_op jit(solution)/shard_map/all_gather | solution.py:81
  187.9 14.1 %collective-permute-start = (bf16[259,1024]{1,0:T(8,128)(2,1)S(1)}, bf16[259,1024]{1,0:T(8,128)(2,1)}, u32[]{:S(2)}, u32[]{:S(2)}) collective-permute-start(bf16[259,1024]{1,0:T(8,128)(2,1)S(1)} %constant_dynamic-slice_fusion.1), channel_id=1, source_target_pairs={{0,4},{4,8},{8,12},{12,16},{16,20},{20,24},{24,28},{28,32},{32,36}... | collective-permute-start | bytes 1591304 | tf_op jit(solution)/shard_map/ppermute | solution.py:10
  190.9 10.3 %collective-permute-start.1 = (bf16[256,1024]{1,0:T(8,128)(2,1)S(1)}, bf16[256,1024]{1,0:T(8,128)(2,1)S(1)}, u32[]{:S(2)}, u32[]{:S(2)}) collective-permute-start(bf16[256,1024]{1,0:T(8,128)(2,1)S(1)} %slice.41), channel_id=1, source_target_pairs={{4,0},{8,4},{12,8},{16,12},{20,16},{24,20},{28,24},{32,28},{36,32}... | collective-permute-start | bytes 1572872 | tf_op jit(solution)/shard_map/ppermute | solution.py:10
  201.2 0.8 copy-start.2
  220.2 1.2 copy-start
  221.4 9.5 %copy-start.5 = (s32[128]{0:T(128)S(1)}, s32[128]{0:T(128)}, u32[]{:S(2)}) copy-start(s32[128]{0:T(128)} %param.10) | copy-start | bytes 1540
  221.4 34.0 %copy-start.3 = (f32[4,1280]{1,0:T(4,128)S(1)}, f32[4,1280]{1,0:T(4,128)}, u32[]{:S(2)}) copy-start(f32[4,1280]{1,0:T(4,128)} %param.12) | copy-start | bytes 61444
  221.7 2.1 copy-start.1
  223.8 29.2 %collective-permute-start.2 = (bf16[515,1024]{1,0:T(8,128)(2,1)S(1)}, bf16[515,1024]{1,0:T(8,128)(2,1)S(1)}, u32[]{:S(2)}, u32[]{:S(2)}) collective-permute-start(bf16[515,1024]{1,0:T(8,128)(2,1)S(1)} %get-tuple-element.98), channel_id=1, source_target_pairs={{0,1},{1,2},{2,3},{3,0},{4,5},{5,6},{6,7},{7,4},{8,9},{9,10},{10,1... | collective-permute-start | bytes 3164168 | tf_op jit(solution)/shard_map/ppermute | solution.py:66
  227.2 29.5 %collective-permute-start.3 = (bf16[515,1024]{1,0:T(8,128)(2,1)S(1)}, bf16[515,1024]{1,0:T(8,128)(2,1)S(1)}, u32[]{:S(2)}, u32[]{:S(2)}) collective-permute-start(bf16[515,1024]{1,0:T(8,128)(2,1)S(1)} %get-tuple-element.98), channel_id=1, source_target_pairs={{0,3},{1,0},{2,1},{3,2},{4,7},{5,4},{6,5},{7,6},{8,11},{9,8},{10,9... | collective-permute-start | bytes 3164168 | tf_op jit(solution)/shard_map/ppermute | solution.py:74
  253.0 28.4 %collective-permute-start.4 = (bf16[515,1024]{1,0:T(8,128)(2,1)S(1)}, bf16[515,1024]{1,0:T(8,128)(2,1)S(1)}, u32[]{:S(2)}, u32[]{:S(2)}) collective-permute-start(bf16[515,1024]{1,0:T(8,128)(2,1)S(1)} %collective-permute-done.2), channel_id=1, source_target_pairs={{0,1},{1,2},{2,3},{3,0},{4,5},{5,6},{6,7},{7,4},{8,9},{9,10},{10,1... | collective-permute-start | bytes 3164168 | tf_op jit(solution)/shard_map/ppermute | solution.py:66
  282.4 11.0 %copy-start.4 = (f32[1280]{0:T(1024)S(1)}, f32[1280]{0:T(1024)}, u32[]{:S(2)}) copy-start(f32[1280]{0:T(1024)} %param.13) | copy-start | bytes 15364
Sparse Core Ops, SparseCore 0:
  10.5 152.7 all-gather.2
